TPU v7x, 512 devices: a whole 4x4x16 slice. The times are simulated.
512 devices in a mesh: lat: 64 (over y, z), lon: 8 (over x, core).
Axes of the slice: x: 4, y: 4, z: 16, core: 2. Of those that a mesh axis runs over, the one named last changes fastest.
Arguments:
- covariance: float32 [64, 64, 128, 128], P('lat', None, 'lon'), may hold values from -6 to 6
- winds: float32 [2, 3, 64, 128], P(None, None, None, 'lon'), may hold values from -0.35 to 0.35
- diffusivity: float32 [64, 128], P(None, 'lon'), may hold values from 0.01 to 0.07
- cutoff: int32 [64], replicated, may hold values from 4 to 16, as said below
Outputs:
- forecast: float32 [64, 64, 128, 128], P('lat', None, 'lon')
Inputs may be any that keep to these rules, and one draw needn't show every extreme that they name: Some latitude has cutoff 16 and some other has 4.
All inputs are finite; a program needn't handle non-finite values.
Results may differ from a plain program's by a relative error of at most 0.00002.
Values sent between devices are 32-bit elements; how exact they have to be, the bound alone decides.
A program may use at most 192 MiB of HBM per device.

v0:
```python
import jax
import jax.numpy as jnp
from jax import lax
from jax.sharding import PartitionSpec as P

STEPS = 3


def extended_2(block, sides, width):
    for axis, dim in sides:
        count = lax.axis_size(axis)
        forward = [(i, i + 1) for i in range(count - 1)]
        forward.append((count - 1, 0))
        backward = [(target, source) for source, target in forward]
        low = lax.ppermute(
            lax.slice_in_dim(block, block.shape[dim] - width, None, axis=dim), axis, forward
        )
        high = lax.ppermute(lax.slice_in_dim(block, 0, width, axis=dim), axis, backward)
        block = jnp.concatenate([low, block, high], axis=dim)
    return block


def from_behind(shard, axis, by):
    length = lax.axis_size(axis)
    pairs = [(i, i + by) for i in range(length) if 0 <= i + by < length]
    return lax.ppermute(shard, axis, pairs)


def advance(extended, east_wind, north_wind, spread):
    center = extended[:, :, 1:-1]
    western = extended[:, :, :-2]
    eastern = extended[:, :, 2:]
    zeros_row = jnp.zeros_like(center[:, :1])
    southern = jnp.concatenate([zeros_row, center[:, :-1]], axis=1)
    northern = jnp.concatenate([center[:, 1:], zeros_row], axis=1)
    east_wind = east_wind[None, :, :, None]
    north_wind = north_wind[None, :, :, None]
    spread = spread[None, :, :, None]
    transport = (
        jnp.maximum(east_wind, 0.0) * (center - western)
        + jnp.minimum(east_wind, 0.0) * (eastern - center)
        + jnp.maximum(north_wind, 0.0) * (center - southern)
        + jnp.minimum(north_wind, 0.0) * (northern - center)
    )
    return center - transport + spread * (eastern + western + northern + southern - 4.0 * center)


def propagate(state_field, winds, diffusivity):
    for substep in range(STEPS):
        extended = extended_2(state_field, (("lon", 2),), 1)
        state_field = advance(extended, winds[0, substep], winds[1, substep], diffusivity)
    return state_field


def relayout(block, reach_rows):
    row_count = block.shape[0]
    lat_count = block.shape[1]
    swapped = lax.all_to_all(block, "lon", split_axis=3, concat_axis=2, tiled=True)
    lon_count = swapped.shape[2]
    col_count = swapped.shape[3]
    block_count = lat_count // row_count
    device_index = lax.axis_index("lat")
    reach_blocks = min((reach_rows + row_count - 1) // row_count, block_count - 1)
    tile_blocks = swapped.reshape(row_count, block_count, row_count, lon_count, col_count)

    def piece_for(offset):
        target = jnp.clip(device_index + offset, 0, block_count - 1)
        return lax.dynamic_index_in_dim(tile_blocks, target, axis=1, keepdims=False)

    own_piece = piece_for(0)
    received = []
    for offset in range(-reach_blocks, reach_blocks + 1):
        if offset == 0:
            received.append(own_piece)
        else:
            received.append(from_behind(piece_for(offset), "lat", offset))
    window = jnp.stack(received[::-1], axis=0)
    padded = jnp.zeros(
        (block_count + 2 * reach_blocks, row_count, row_count, lon_count, col_count), jnp.float32
    )
    padded = lax.dynamic_update_slice_in_dim(padded, window, device_index, 0)
    regrouped = padded[reach_blocks : reach_blocks + block_count].reshape(
        lat_count, row_count, lon_count, col_count
    )
    return jnp.transpose(regrouped, (1, 0, 3, 2))


def per_device(covariance, winds, diffusivity, cutoff):
    row_count = covariance.shape[0]
    lat_count = covariance.shape[1]
    band_rows = lat_count // 4
    device_index = lax.axis_index("lat")
    lat_local = device_index * row_count + jnp.arange(row_count, dtype=jnp.int32)
    lat_all = jnp.arange(lat_count, dtype=jnp.int32)
    cut_local = lax.dynamic_slice_in_dim(cutoff, device_index * row_count, row_count)
    keep_first = jnp.abs(lat_all[None, :] - lat_local[:, None]) <= cutoff[None, :]
    keep_second = jnp.abs(lat_all[None, :] - lat_local[:, None]) <= cut_local[:, None]
    state_field = jnp.where(keep_first[:, :, None, None], covariance, 0.0)
    state_field = propagate(state_field, winds, diffusivity)
    state_field = relayout(state_field, band_rows + STEPS)
    state_field = propagate(state_field, winds, diffusivity)
    state_field = jnp.where(keep_second[:, :, None, None], state_field, 0.0)
    return relayout(state_field, band_rows)


def solution(mesh):
    in_specs = (P("lat", None, "lon", None), P(None, None, None, "lon"), P(None, "lon"), P())
    out_specs = P("lat", None, "lon", None)
    return jax.shard_map(
        per_device, mesh=mesh, in_specs=in_specs, out_specs=out_specs, check_vma=False
    )
```

profile of v0, /device:TPU:24, one launch (start us, length us, event | category | flops | bytes accessed | tf_op | source)
XLA Modules:
  0.0 880.4 jit_solution(16110254045664270610)
XLA Ops:
  28.5 10.3 %all-to-all-done = f32[8,1,16384]{2,1,0:T(1,128)S(1)} async-done(((f32[8,1,16384]{2,1,0:T(1,128)}), f32[8,1,16384]{2,1,0:T(1,128)S(1)}, u32[]{:S(2)}, u32[]{:S(2)}) %all-to-all-start) | async-done | bytes 524320 | tf_op jit(solution)/shard_map/all_to_all | solution.py:58
  44.4 8.4 constant_dynamic-slice_fusion.51
  54.4 21.2 %collective-permute-start.7 = (f32[1,1,128,16]{2,3,1,0:T(8,128)S(1)}, f32[1,1,128,16]{2,3,1,0:T(8,128)S(1)}, u32[]{:S(2)}, u32[]{:S(2)}) collective-permute-start(f32[1,1,128,16]{2,3,1,0:T(8,128)S(1)} %bitcast.330), channel_id=1, source_target_pairs={{0,144},{8,152},{16,160},{24,168},{32,176},{40,184},{48,192},{56,2... | collective-permute-start | bytes 24584 | tf_op jit(solution)/shard_map/ppermute | solution.py:26
  77.3 19.0 %collective-permute-start.8 = (f32[1,1,128,16]{2,3,1,0:T(8,128)S(1)}, f32[1,1,128,16]{2,3,1,0:T(8,128)S(1)}, u32[]{:S(2)}, u32[]{:S(2)}) collective-permute-start(f32[1,1,128,16]{2,3,1,0:T(8,128)S(1)} %bitcast.329), channel_id=1, source_target_pairs={{0,136},{8,144},{16,152},{24,160},{32,168},{40,176},{48,184},{56,1... | collective-permute-start | bytes 24584 | tf_op jit(solution)/shard_map/ppermute | solution.py:26
  100.8 8.6 collective-permute-start.10
  143.9 8.9 %constant_dynamic-slice_fusion.32 = (f32[1,1,1,128,16]{1,4,3,2,0:T(8,128)}, f32[1,1,1,128,16]{1,4,3,2,0:T(8,128)}, f32[1,1,1,128,16]{1,4,3,2,0:T(8,128)}, f32[1,...) fusion(f32[1,64,1,128,16]{1,4,3,2,0:T(8,128)S(1)} %bitcast.189,, ...), kind=kLoop, calls=%fused_computation.205 | loop fusion | bytes 294984 | tf_op jit(solution)/shard_map/jit(dynamic_index_in_dim)/dynamic_slice | solution.py:68
  222.6 6.4 collective-permute-start.26
  231.1 6.9 collective-permute-start.27
  239.4 7.8 collective-permute-start.28
  248.6 8.7 collective-permute-start.29
  295.2 10.0 %collective-permute-start.30 = (f32[1,1,128,16]{2,3,1,0:T(8,128)S(1)}, f32[1,1,128,16]{2,3,1,0:T(8,128)S(1)}, u32[]{:S(2)}, u32[]{:S(2)}) collective-permute-start(f32[1,1,128,16]{2,3,1,0:T(8,128)S(1)} %bitcast.218), channel_id=1, source_target_pairs={{48,0},{56,8},{64,16},{72,24},{80,32},{88,40},{96,48},{104,56},{11... | collective-permute-start | bytes 24584 | tf_op jit(solution)/shard_map/ppermute | solution.py:26
  305.7 11.5 %collective-permute-start.31 = (f32[1,1,128,16]{2,3,1,0:T(8,128)S(1)}, f32[1,1,128,16]{2,3,1,0:T(8,128)S(1)}, u32[]{:S(2)}, u32[]{:S(2)}) collective-permute-start(f32[1,1,128,16]{2,3,1,0:T(8,128)S(1)} %bitcast.217), channel_id=1, source_target_pairs={{56,0},{64,8},{72,16},{80,24},{88,32},{96,40},{104,48},{112,56},{1... | collective-permute-start | bytes 24584 | tf_op jit(solution)/shard_map/ppermute | solution.py:26
  317.2 12.4 %collective-permute-start.32 = (f32[1,1,128,16]{2,3,1,0:T(8,128)S(1)}, f32[1,1,128,16]{2,3,1,0:T(8,128)S(1)}, u32[]{:S(2)}, u32[]{:S(2)}) collective-permute-start(f32[1,1,128,16]{2,3,1,0:T(8,128)S(1)} %bitcast.216), channel_id=1, source_target_pairs={{64,0},{72,8},{80,16},{88,24},{96,32},{104,40},{112,48},{120,56},{... | collective-permute-start | bytes 24584 | tf_op jit(solution)/shard_map/ppermute | solution.py:26
  329.6 10.3 %collective-permute-start.33 = (f32[1,1,128,16]{2,3,1,0:T(8,128)S(1)}, f32[1,1,128,16]{2,3,1,0:T(8,128)S(1)}, u32[]{:S(2)}, u32[]{:S(2)}) collective-permute-start(f32[1,1,128,16]{2,3,1,0:T(8,128)S(1)} %bitcast.215), channel_id=1, source_target_pairs={{72,0},{80,8},{88,16},{96,24},{104,32},{112,40},{120,48},{128,56},... | collective-permute-start | bytes 24584 | tf_op jit(solution)/shard_map/ppermute | solution.py:26
  357.7 13.2 %collective-permute-start.41 = (f32[1,1,128,16]{2,3,1,0:T(8,128)S(1)}, f32[1,1,128,16]{2,3,1,0:T(8,128)S(1)}, u32[]{:S(2)}, u32[]{:S(2)}) collective-permute-start(f32[1,1,128,16]{2,3,1,0:T(8,128)S(1)} %bitcast.199), channel_id=1, source_target_pairs={{136,0},{144,8},{152,16},{160,24},{168,32},{176,40},{184,48},{192,... | collective-permute-start | bytes 24584 | tf_op jit(solution)/shard_map/ppermute | solution.py:26
  371.0 19.0 %collective-permute-start.42 = (f32[1,1,128,16]{2,3,1,0:T(8,128)S(1)}, f32[1,1,128,16]{2,3,1,0:T(8,128)S(1)}, u32[]{:S(2)}, u32[]{:S(2)}) collective-permute-start(f32[1,1,128,16]{2,3,1,0:T(8,128)S(1)} %bitcast.198), channel_id=1, source_target_pairs={{144,0},{152,8},{160,16},{168,24},{176,32},{184,40},{192,48},{200,... | collective-permute-start | bytes 24584 | tf_op jit(solution)/shard_map/ppermute | solution.py:26
  390.0 19.0 %collective-permute-start.43 = (f32[1,1,128,16]{2,3,1,0:T(8,128)S(1)}, f32[1,1,128,16]{2,3,1,0:T(8,128)S(1)}, u32[]{:S(2)}, u32[]{:S(2)}) collective-permute-start(f32[1,1,128,16]{2,3,1,0:T(8,128)S(1)} %bitcast.197), channel_id=1, source_target_pairs={{152,0},{160,8},{168,16},{176,24},{184,32},{192,40},{200,48},{208,... | collective-permute-start | bytes 24584 | tf_op jit(solution)/shard_map/ppermute | solution.py:26
  409.0 9.1 %collective-permute-start.25 = (f32[1,1,128,16]{2,3,1,0:T(8,128)S(1)}, f32[1,1,128,16]{2,3,1,0:T(8,128)S(1)}, u32[]{:S(2)}, u32[]{:S(2)}) collective-permute-start(f32[1,1,128,16]{2,3,1,0:T(8,128)S(1)} %bitcast.265), channel_id=1, source_target_pairs={{8,0},{16,8},{24,16},{32,24},{40,32},{48,40},{56,48},{64,56},{72,6... | collective-permute-start | bytes 24584 | tf_op jit(solution)/shard_map/ppermute | solution.py:26
  482.8 23.8 %copy.588 = f32[39,1,1,128,16]{0,4,3,2,1:T(8,128)S(1)} copy(f32[39,1,1,128,16]{1,4,3,2,0:T(8,128)} %constant_dynamic-update-slice_fusion) | data formatting | bytes 638976 | tf_op jit(solution)/shard_map/stack | solution.py:77
  506.6 21.2 %dynamic_update_slice.6 = f32[102,1,1,128,16]{0,4,3,2,1:T(8,128)S(1)} dynamic-update-slice(f32[102,1,1,128,16]{0,4,3,2,1:T(8,128)S(1)} %broadcast_in_dim.38, f32[39,1,1,128,16]{0,4,3,2,1:T(8,128)S(1)} %copy.588, s32[]{:T(128)S(6)} %select_n.91, s32[]{:T(128)} %constant.241.clone.1, s32[]{:T(128)} %constant.241.clone.1, s32[]{:T(128)} %constant.241.clone.1, s32[]{:T(128)} %constant.241.clone.1) | dynamic-update-slice | bytes 638980 | tf_op jit(solution)/shard_map/dynamic_update_slice | solution.py:81
  547.2 14.6 %all_to_all.30 = f32[8,1,16384]{2,1,0:T(1,128)S(1)} all-to-all(f32[8,1,16384]{2,1,0:T(1,128)S(1)} %reshape.178), channel_id=1, replica_groups=mesh['lat'=64,'lon'=8] {'lon'}, dimensions={0} | all-to-all | bytes 1048576 | tf_op jit(solution)/shard_map/all_to_all | solution.py:58
  564.6 7.4 constant_dynamic-slice_fusion.16
  684.9 7.9 constant_dynamic-slice_fusion
  694.4 5.5 collective-permute-start.66
  707.9 6.8 collective-permute-start.68
  716.4 7.4 collective-permute-start.69
  725.4 8.7 collective-permute-start.70
  735.8 12.0 %collective-permute-start.71 = (f32[1,1,128,16]{2,3,1,0:T(8,128)S(1)}, f32[1,1,128,16]{2,3,1,0:T(8,128)S(1)}, u32[]{:S(2)}, u32[]{:S(2)}) collective-permute-start(f32[1,1,128,16]{2,3,1,0:T(8,128)S(1)} %bitcast.320), channel_id=1, source_target_pairs={{48,0},{56,8},{64,16},{72,24},{80,32},{88,40},{96,48},{104,56},{11... | collective-permute-start | bytes 24584 | tf_op jit(solution)/shard_map/ppermute | solution.py:26
  755.9 9.7 %collective-permute-start.72 = (f32[1,1,128,16]{2,3,1,0:T(8,128)S(1)}, f32[1,1,128,16]{2,3,1,0:T(8,128)S(1)}, u32[]{:S(2)}, u32[]{:S(2)}) collective-permute-start(f32[1,1,128,16]{2,3,1,0:T(8,128)S(1)} %bitcast.311), channel_id=1, source_target_pairs={{56,0},{64,8},{72,16},{80,24},{88,32},{96,40},{104,48},{112,56},{1... | collective-permute-start | bytes 24584 | tf_op jit(solution)/shard_map/ppermute | solution.py:26
  765.6 12.4 %collective-permute-start.73 = (f32[1,1,128,16]{2,3,1,0:T(8,128)S(1)}, f32[1,1,128,16]{2,3,1,0:T(8,128)S(1)}, u32[]{:S(2)}, u32[]{:S(2)}) collective-permute-start(f32[1,1,128,16]{2,3,1,0:T(8,128)S(1)} %bitcast.304), channel_id=1, source_target_pairs={{64,0},{72,8},{80,16},{88,24},{96,32},{104,40},{112,48},{120,56},{... | collective-permute-start | bytes 24584 | tf_op jit(solution)/shard_map/ppermute | solution.py:26
  778.0 10.1 %collective-permute-start.74 = (f32[1,1,128,16]{2,3,1,0:T(8,128)S(1)}, f32[1,1,128,16]{2,3,1,0:T(8,128)S(1)}, u32[]{:S(2)}, u32[]{:S(2)}) collective-permute-start(f32[1,1,128,16]{2,3,1,0:T(8,128)S(1)} %bitcast.299), channel_id=1, source_target_pairs={{72,0},{80,8},{88,16},{96,24},{104,32},{112,40},{120,48},{128,56},... | collective-permute-start | bytes 24584 | tf_op jit(solution)/shard_map/ppermute | solution.py:26
  860.0 19.0 %copy.655 = f32[33,1,1,128,16]{3,4,0,2,1:T(8,128)S(1)} copy(f32[33,1,1,128,16]{1,4,3,2,0:T(8,128)} %constant_dynamic-update-slice_fusion.38) | data formatting | bytes 540672 | tf_op jit(solution)/shard_map/stack | solution.py:77
  (398 shorter events, 501.4 us)
Async XLA Ops:
  42.9 71.4 %collective-permute-start.6 = (f32[1,1,128,16]{2,3,1,0:T(8,128)S(1)}, f32[1,1,128,16]{2,3,1,0:T(8,128)S(1)}, u32[]{:S(2)}, u32[]{:S(2)}) collective-permute-start(f32[1,1,128,16]{2,3,1,0:T(8,128)S(1)} %bitcast.315), channel_id=1, source_target_pairs={{0,152},{8,160},{16,168},{24,176},{32,184},{40,192},{48,200},{56,2... | collective-permute-start | bytes 24584 | tf_op jit(solution)/shard_map/ppermute | solution.py:26
  54.4 61.8 %collective-permute-start.7 = (f32[1,1,128,16]{2,3,1,0:T(8,128)S(1)}, f32[1,1,128,16]{2,3,1,0:T(8,128)S(1)}, u32[]{:S(2)}, u32[]{:S(2)}) collective-permute-start(f32[1,1,128,16]{2,3,1,0:T(8,128)S(1)} %bitcast.330), channel_id=1, source_target_pairs={{0,144},{8,152},{16,160},{24,168},{32,176},{40,184},{48,192},{56,2... | collective-permute-start | bytes 24584 | tf_op jit(solution)/shard_map/ppermute | solution.py:26
  77.3 40.9 %collective-permute-start.8 = (f32[1,1,128,16]{2,3,1,0:T(8,128)S(1)}, f32[1,1,128,16]{2,3,1,0:T(8,128)S(1)}, u32[]{:S(2)}, u32[]{:S(2)}) collective-permute-start(f32[1,1,128,16]{2,3,1,0:T(8,128)S(1)} %bitcast.329), channel_id=1, source_target_pairs={{0,136},{8,144},{16,152},{24,160},{32,168},{40,176},{48,184},{56,1... | collective-permute-start | bytes 24584 | tf_op jit(solution)/shard_map/ppermute | solution.py:26
  130.2 61.2 %collective-permute-start.14 = (f32[1,1,128,16]{2,3,1,0:T(8,128)}, f32[1,1,128,16]{2,3,1,0:T(8,128)S(1)}, u32[]{:S(2)}, u32[]{:S(2)}) collective-permute-start(f32[1,1,128,16]{2,3,1,0:T(8,128)} %bitcast.32), channel_id=1, source_target_pairs={{0,88},{8,96},{16,104},{24,112},{32,120},{40,128},{48,136},{56,144... | collective-permute-start | bytes 24584 | tf_op jit(solution)/shard_map/ppermute | solution.py:26
  133.3 60.1 %collective-permute-start.15 = (f32[1,1,128,16]{2,3,1,0:T(8,128)}, f32[1,1,128,16]{2,3,1,0:T(8,128)S(1)}, u32[]{:S(2)}, u32[]{:S(2)}) collective-permute-start(f32[1,1,128,16]{2,3,1,0:T(8,128)} %bitcast.34), channel_id=1, source_target_pairs={{0,80},{8,88},{16,96},{24,104},{32,112},{40,120},{48,128},{56,136}... | collective-permute-start | bytes 24584 | tf_op jit(solution)/shard_map/ppermute | solution.py:26
  135.2 60.1 %collective-permute-start.16 = (f32[1,1,128,16]{2,3,1,0:T(8,128)S(1)}, f32[1,1,128,16]{2,3,1,0:T(8,128)S(1)}, u32[]{:S(2)}, u32[]{:S(2)}) collective-permute-start(f32[1,1,128,16]{2,3,1,0:T(8,128)S(1)} %bitcast.245), channel_id=1, source_target_pairs={{0,72},{8,80},{16,88},{24,96},{32,104},{40,112},{48,120},{56,128},... | collective-permute-start | bytes 24584 | tf_op jit(solution)/shard_map/ppermute | solution.py:26
  137.2 60.1 %collective-permute-start.17 = (f32[1,1,128,16]{2,3,1,0:T(8,128)S(1)}, f32[1,1,128,16]{2,3,1,0:T(8,128)S(1)}, u32[]{:S(2)}, u32[]{:S(2)}) collective-permute-start(f32[1,1,128,16]{2,3,1,0:T(8,128)S(1)} %bitcast.239), channel_id=1, source_target_pairs={{0,64},{8,72},{16,80},{24,88},{32,96},{40,104},{48,112},{56,120},{... | collective-permute-start | bytes 24584 | tf_op jit(solution)/shard_map/ppermute | solution.py:26
  139.1 60.7 %collective-permute-start.18 = (f32[1,1,128,16]{2,3,1,0:T(8,128)S(1)}, f32[1,1,128,16]{2,3,1,0:T(8,128)S(1)}, u32[]{:S(2)}, u32[]{:S(2)}) collective-permute-start(f32[1,1,128,16]{2,3,1,0:T(8,128)S(1)} %bitcast.237), channel_id=1, source_target_pairs={{0,56},{8,64},{16,72},{24,80},{32,88},{40,96},{48,104},{56,112},{6... | collective-permute-start | bytes 24584 | tf_op jit(solution)/shard_map/ppermute | solution.py:26
  195.4 35.7 %collective-permute-start.21 = (f32[1,1,128,16]{2,3,1,0:T(8,128)S(1)}, f32[1,1,128,16]{2,3,1,0:T(8,128)S(1)}, u32[]{:S(2)}, u32[]{:S(2)}) collective-permute-start(f32[1,1,128,16]{2,3,1,0:T(8,128)S(1)} %bitcast.247), channel_id=1, source_target_pairs={{0,32},{8,40},{16,48},{24,56},{32,64},{40,72},{48,80},{56,88},{64,... | collective-permute-start | bytes 24584 | tf_op jit(solution)/shard_map/ppermute | solution.py:26
  197.3 42.1 %collective-permute-start.22 = (f32[1,1,128,16]{2,3,1,0:T(8,128)S(1)}, f32[1,1,128,16]{2,3,1,0:T(8,128)S(1)}, u32[]{:S(2)}, u32[]{:S(2)}) collective-permute-start(f32[1,1,128,16]{2,3,1,0:T(8,128)S(1)} %bitcast.240), channel_id=1, source_target_pairs={{0,24},{8,32},{16,40},{24,48},{32,56},{40,64},{48,72},{56,80},{64,... | collective-permute-start | bytes 24584 | tf_op jit(solution)/shard_map/ppermute | solution.py:26
  199.8 48.8 %collective-permute-start.23 = (f32[1,1,128,16]{2,3,1,0:T(8,128)S(1)}, f32[1,1,128,16]{2,3,1,0:T(8,128)S(1)}, u32[]{:S(2)}, u32[]{:S(2)}) collective-permute-start(f32[1,1,128,16]{2,3,1,0:T(8,128)S(1)} %bitcast.236), channel_id=1, source_target_pairs={{0,16},{8,24},{16,32},{24,40},{32,48},{40,56},{48,64},{56,72},{64,... | collective-permute-start | bytes 24584 | tf_op jit(solution)/shard_map/ppermute | solution.py:26
  218.0 77.2 %collective-permute-start.24 = (f32[1,1,128,16]{2,3,1,0:T(8,128)S(1)}, f32[1,1,128,16]{2,3,1,0:T(8,128)S(1)}, u32[]{:S(2)}, u32[]{:S(2)}) collective-permute-start(f32[1,1,128,16]{2,3,1,0:T(8,128)S(1)} %bitcast.225), channel_id=1, source_target_pairs={{0,8},{8,16},{16,24},{24,32},{32,40},{40,48},{48,56},{56,64},{64,7... | collective-permute-start | bytes 24584 | tf_op jit(solution)/shard_map/ppermute | solution.py:26
  222.6 83.2 %collective-permute-start.26 = (f32[1,1,128,16]{2,3,1,0:T(8,128)S(1)}, f32[1,1,128,16]{2,3,1,0:T(8,128)S(1)}, u32[]{:S(2)}, u32[]{:S(2)}) collective-permute-start(f32[1,1,128,16]{2,3,1,0:T(8,128)S(1)} %bitcast.223), channel_id=1, source_target_pairs={{16,0},{24,8},{32,16},{40,24},{48,32},{56,40},{64,48},{72,56},{80,... | collective-permute-start | bytes 24584 | tf_op jit(solution)/shard_map/ppermute | solution.py:26
  231.1 86.1 %collective-permute-start.27 = (f32[1,1,128,16]{2,3,1,0:T(8,128)S(1)}, f32[1,1,128,16]{2,3,1,0:T(8,128)S(1)}, u32[]{:S(2)}, u32[]{:S(2)}) collective-permute-start(f32[1,1,128,16]{2,3,1,0:T(8,128)S(1)} %bitcast.222), channel_id=1, source_target_pairs={{24,0},{32,8},{40,16},{48,24},{56,32},{64,40},{72,48},{80,56},{88,... | collective-permute-start | bytes 24584 | tf_op jit(solution)/shard_map/ppermute | solution.py:26
  239.4 90.2 %collective-permute-start.28 = (f32[1,1,128,16]{2,3,1,0:T(8,128)S(1)}, f32[1,1,128,16]{2,3,1,0:T(8,128)S(1)}, u32[]{:S(2)}, u32[]{:S(2)}) collective-permute-start(f32[1,1,128,16]{2,3,1,0:T(8,128)S(1)} %bitcast.220), channel_id=1, source_target_pairs={{32,0},{40,8},{48,16},{56,24},{64,32},{72,40},{80,48},{88,56},{96,... | collective-permute-start | bytes 24584 | tf_op jit(solution)/shard_map/ppermute | solution.py:26
  248.6 91.3 %collective-permute-start.29 = (f32[1,1,128,16]{2,3,1,0:T(8,128)S(1)}, f32[1,1,128,16]{2,3,1,0:T(8,128)S(1)}, u32[]{:S(2)}, u32[]{:S(2)}) collective-permute-start(f32[1,1,128,16]{2,3,1,0:T(8,128)S(1)} %bitcast.219), channel_id=1, source_target_pairs={{40,0},{48,8},{56,16},{64,24},{72,32},{80,40},{88,48},{96,56},{104... | collective-permute-start | bytes 24584 | tf_op jit(solution)/shard_map/ppermute | solution.py:26
  295.2 48.5 %collective-permute-start.30 = (f32[1,1,128,16]{2,3,1,0:T(8,128)S(1)}, f32[1,1,128,16]{2,3,1,0:T(8,128)S(1)}, u32[]{:S(2)}, u32[]{:S(2)}) collective-permute-start(f32[1,1,128,16]{2,3,1,0:T(8,128)S(1)} %bitcast.218), channel_id=1, source_target_pairs={{48,0},{56,8},{64,16},{72,24},{80,32},{88,40},{96,48},{104,56},{11... | collective-permute-start | bytes 24584 | tf_op jit(solution)/shard_map/ppermute | solution.py:26
  305.7 39.9 %collective-permute-start.31 = (f32[1,1,128,16]{2,3,1,0:T(8,128)S(1)}, f32[1,1,128,16]{2,3,1,0:T(8,128)S(1)}, u32[]{:S(2)}, u32[]{:S(2)}) collective-permute-start(f32[1,1,128,16]{2,3,1,0:T(8,128)S(1)} %bitcast.217), channel_id=1, source_target_pairs={{56,0},{64,8},{72,16},{80,24},{88,32},{96,40},{104,48},{112,56},{1... | collective-permute-start | bytes 24584 | tf_op jit(solution)/shard_map/ppermute | solution.py:26
  349.5 40.5 %collective-permute-start.38 = (f32[1,1,128,16]{2,3,1,0:T(8,128)S(1)}, f32[1,1,128,16]{2,3,1,0:T(8,128)S(1)}, u32[]{:S(2)}, u32[]{:S(2)}) collective-permute-start(f32[1,1,128,16]{2,3,1,0:T(8,128)S(1)} %bitcast.210), channel_id=1, source_target_pairs={{112,0},{120,8},{128,16},{136,24},{144,32},{152,40},{160,48},{168,... | collective-permute-start | bytes 24584 | tf_op jit(solution)/shard_map/ppermute | solution.py:26
  352.4 56.6 %collective-permute-start.39 = (f32[1,1,128,16]{2,3,1,0:T(8,128)S(1)}, f32[1,1,128,16]{2,3,1,0:T(8,128)S(1)}, u32[]{:S(2)}, u32[]{:S(2)}) collective-permute-start(f32[1,1,128,16]{2,3,1,0:T(8,128)S(1)} %bitcast.209), channel_id=1, source_target_pairs={{120,0},{128,8},{136,16},{144,24},{152,32},{160,40},{168,48},{176,... | collective-permute-start | bytes 24584 | tf_op jit(solution)/shard_map/ppermute | solution.py:26
  356.4 79.4 %collective-permute-start.40 = (f32[1,1,128,16]{2,3,1,0:T(8,128)S(1)}, f32[1,1,128,16]{2,3,1,0:T(8,128)S(1)}, u32[]{:S(2)}, u32[]{:S(2)}) collective-permute-start(f32[1,1,128,16]{2,3,1,0:T(8,128)S(1)} %bitcast.200), channel_id=1, source_target_pairs={{128,0},{136,8},{144,16},{152,24},{160,32},{168,40},{176,48},{184,... | collective-permute-start | bytes 24584 | tf_op jit(solution)/shard_map/ppermute | solution.py:26
  357.7 79.6 %collective-permute-start.41 = (f32[1,1,128,16]{2,3,1,0:T(8,128)S(1)}, f32[1,1,128,16]{2,3,1,0:T(8,128)S(1)}, u32[]{:S(2)}, u32[]{:S(2)}) collective-permute-start(f32[1,1,128,16]{2,3,1,0:T(8,128)S(1)} %bitcast.199), channel_id=1, source_target_pairs={{136,0},{144,8},{152,16},{160,24},{168,32},{176,40},{184,48},{192,... | collective-permute-start | bytes 24584 | tf_op jit(solution)/shard_map/ppermute | solution.py:26
  371.0 67.7 %collective-permute-start.42 = (f32[1,1,128,16]{2,3,1,0:T(8,128)S(1)}, f32[1,1,128,16]{2,3,1,0:T(8,128)S(1)}, u32[]{:S(2)}, u32[]{:S(2)}) collective-permute-start(f32[1,1,128,16]{2,3,1,0:T(8,128)S(1)} %bitcast.198), channel_id=1, source_target_pairs={{144,0},{152,8},{160,16},{168,24},{176,32},{184,40},{192,48},{200,... | collective-permute-start | bytes 24584 | tf_op jit(solution)/shard_map/ppermute | solution.py:26
  390.0 50.1 %collective-permute-start.43 = (f32[1,1,128,16]{2,3,1,0:T(8,128)S(1)}, f32[1,1,128,16]{2,3,1,0:T(8,128)S(1)}, u32[]{:S(2)}, u32[]{:S(2)}) collective-permute-start(f32[1,1,128,16]{2,3,1,0:T(8,128)S(1)} %bitcast.197), channel_id=1, source_target_pairs={{152,0},{160,8},{168,16},{176,24},{184,32},{192,40},{200,48},{208,... | collective-permute-start | bytes 24584 | tf_op jit(solution)/shard_map/ppermute | solution.py:26
  694.4 41.4 %collective-permute-start.66 = (f32[1,1,128,16]{2,3,1,0:T(8,128)S(1)}, f32[1,1,128,16]{2,3,1,0:T(8,128)S(1)}, u32[]{:S(2)}, u32[]{:S(2)}) collective-permute-start(f32[1,1,128,16]{2,3,1,0:T(8,128)S(1)} %bitcast.332), channel_id=1, source_target_pairs={{8,0},{16,8},{24,16},{32,24},{40,32},{48,40},{56,48},{64,56},{72,6... | collective-permute-start | bytes 24584 | tf_op jit(solution)/shard_map/ppermute | solution.py:26
  701.5 54.4 %collective-permute-start.67 = (f32[1,1,128,16]{2,3,1,0:T(8,128)S(1)}, f32[1,1,128,16]{2,3,1,0:T(8,128)S(1)}, u32[]{:S(2)}, u32[]{:S(2)}) collective-permute-start(f32[1,1,128,16]{2,3,1,0:T(8,128)S(1)} %bitcast.328), channel_id=1, source_target_pairs={{16,0},{24,8},{32,16},{40,24},{48,32},{56,40},{64,48},{72,56},{80,... | collective-permute-start | bytes 24584 | tf_op jit(solution)/shard_map/ppermute | solution.py:26
  707.9 57.7 %collective-permute-start.68 = (f32[1,1,128,16]{2,3,1,0:T(8,128)S(1)}, f32[1,1,128,16]{2,3,1,0:T(8,128)S(1)}, u32[]{:S(2)}, u32[]{:S(2)}) collective-permute-start(f32[1,1,128,16]{2,3,1,0:T(8,128)S(1)} %bitcast.326), channel_id=1, source_target_pairs={{24,0},{32,8},{40,16},{48,24},{56,32},{64,40},{72,48},{80,56},{88,... | collective-permute-start | bytes 24584 | tf_op jit(solution)/shard_map/ppermute | solution.py:26
  716.4 61.6 %collective-permute-start.69 = (f32[1,1,128,16]{2,3,1,0:T(8,128)S(1)}, f32[1,1,128,16]{2,3,1,0:T(8,128)S(1)}, u32[]{:S(2)}, u32[]{:S(2)}) collective-permute-start(f32[1,1,128,16]{2,3,1,0:T(8,128)S(1)} %bitcast.324), channel_id=1, source_target_pairs={{32,0},{40,8},{48,16},{56,24},{64,32},{72,40},{80,48},{88,56},{96,... | collective-permute-start | bytes 24584 | tf_op jit(solution)/shard_map/ppermute | solution.py:26
  725.4 62.7 %collective-permute-start.70 = (f32[1,1,128,16]{2,3,1,0:T(8,128)S(1)}, f32[1,1,128,16]{2,3,1,0:T(8,128)S(1)}, u32[]{:S(2)}, u32[]{:S(2)}) collective-permute-start(f32[1,1,128,16]{2,3,1,0:T(8,128)S(1)} %bitcast.322), channel_id=1, source_target_pairs={{40,0},{48,8},{56,16},{64,24},{72,32},{80,40},{88,48},{96,56},{104... | collective-permute-start | bytes 24584 | tf_op jit(solution)/shard_map/ppermute | solution.py:26
  735.8 54.4 %collective-permute-start.71 = (f32[1,1,128,16]{2,3,1,0:T(8,128)S(1)}, f32[1,1,128,16]{2,3,1,0:T(8,128)S(1)}, u32[]{:S(2)}, u32[]{:S(2)}) collective-permute-start(f32[1,1,128,16]{2,3,1,0:T(8,128)S(1)} %bitcast.320), channel_id=1, source_target_pairs={{48,0},{56,8},{64,16},{72,24},{80,32},{88,40},{96,48},{104,56},{11... | collective-permute-start | bytes 24584 | tf_op jit(solution)/shard_map/ppermute | solution.py:26
  755.9 42.0 %collective-permute-start.72 = (f32[1,1,128,16]{2,3,1,0:T(8,128)S(1)}, f32[1,1,128,16]{2,3,1,0:T(8,128)S(1)}, u32[]{:S(2)}, u32[]{:S(2)}) collective-permute-start(f32[1,1,128,16]{2,3,1,0:T(8,128)S(1)} %bitcast.311), channel_id=1, source_target_pairs={{56,0},{64,8},{72,16},{80,24},{88,32},{96,40},{104,48},{112,56},{1... | collective-permute-start | bytes 24584 | tf_op jit(solution)/shard_map/ppermute | solution.py:26
  765.6 34.2 %collective-permute-start.73 = (f32[1,1,128,16]{2,3,1,0:T(8,128)S(1)}, f32[1,1,128,16]{2,3,1,0:T(8,128)S(1)}, u32[]{:S(2)}, u32[]{:S(2)}) collective-permute-start(f32[1,1,128,16]{2,3,1,0:T(8,128)S(1)} %bitcast.304), channel_id=1, source_target_pairs={{64,0},{72,8},{80,16},{88,24},{96,32},{104,40},{112,48},{120,56},{... | collective-permute-start | bytes 24584 | tf_op jit(solution)/shard_map/ppermute | solution.py:26
  (53 other events, 1091.7 us)
where the time goes:
time: 895 us; the launch traced here: 880 us
  local copies, waits for them, and re-layouts  449 us (50%)
  starting transfers between devices  380 us (42%)
  waiting for transfers between devices  20.2 us (2%)
  other arithmetic  14.6 us (2%)
  blocking collectives  14.6 us (2%)
    ppermute x70, starting transfers between devices, from_behind(): return lax.ppermute(shard, axis, pairs)  358 us
    unnamed x77, local copies, waits for them, and re-layouts  144 us
    dynamic_slice x76, local copies, waits for them, and re-layouts, piece_for(): return lax.dynamic_index_in_dim(tile_blocks, target, axis=1, keepdims=False)  142 us
    another operation x74, local copies, waits for them, and re-layouts, relayout(): window = jnp.stack(received[::-1], axis=0)  136 us
    dynamic_update_slice x2, local copies, waits for them, and re-layouts, relayout(): padded = lax.dynamic_update_slice_in_dim(padded, window, device_index, 0)  21.2 us
  transfers between devices with their start and end apart: 83, of which 8 were waited for; matrix products, arithmetic and copies ran while one was open for 28% of the time, Pallas kernels for 0%

commit v1 on v0

--- a/solution.py
+++ b/solution.py
@@ -4,6 +4,30 @@
 from jax.sharding import PartitionSpec as P
 
 STEPS = 3
+
+
+def cut_along(value, dim, size):
+    shape = value.shape
+    blocks = value.reshape(*shape[:dim], size, shape[dim] // size, *shape[dim + 1 :])
+    return jnp.moveaxis(blocks, dim, 0)
+
+
+def joined_along(blocks, dim):
+    blocks = jnp.moveaxis(blocks, 0, dim)
+    shape = blocks.shape
+    return blocks.reshape(*shape[:dim], shape[dim] * shape[dim + 1], *shape[dim + 2 :])
+
+
+def rotated_exchange(x, axis, split_dim, concat_dim):
+    size, place = (lax.axis_size(axis), lax.axis_index(axis))
+    blocks = cut_along(x, split_dim, size)
+    whole = blocks
+    for step in range(1, size):
+        target, source = ((place + step) % size, (place - step) % size)
+        sent = lax.dynamic_index_in_dim(blocks, target, 0)
+        other = lax.ppermute(sent, axis, [(i, (i + step) % size) for i in range(size)])
+        whole = lax.dynamic_update_slice_in_dim(whole, other, source, axis=0)
+    return joined_along(whole, concat_dim)
 
 
 def extended_2(block, sides, width):
@@ -55,7 +79,7 @@
 def relayout(block, reach_rows):
     row_count = block.shape[0]
     lat_count = block.shape[1]
-    swapped = lax.all_to_all(block, "lon", split_axis=3, concat_axis=2, tiled=True)
+    swapped = rotated_exchange(block, "lon", 3, 2)
     lon_count = swapped.shape[2]
     col_count = swapped.shape[3]
     block_count = lat_count // row_count

time: 895 us -> 928 us (1.037)
  starting transfers between devices: 380 us -> 515 us
  local copies, waits for them, and re-layouts: 449 us -> 370 us
  blocking collectives: 14.6 us -> 0 us
    ppermute x0 -> x14, starting transfers between devices: none -> 133 us  [rotated_exchange(): lax.ppermute(sent, axis, [(i, (i + step) % size) for i in range(size)])]
    unnamed x77 -> x39, local copies, waits for them, and re-layouts: 144 us -> 76.7 us
    all_to_all x1 -> x0, blocking collectives: 14.6 us -> none  [relayout(): lax.all_to_all(block, 'lon', split_axis=3, concat_axis=2, tiled=True)]
    dynamic_update_slice x2, local copies, waits for them, and re-layouts: 21.2 us -> 7.18 us  [relayout(): padded = lax.dynamic_update_slice_in_dim(padded, window, device_index, 0)]
    all_to_all x1 -> x0, waiting for transfers between devices: 10.3 us -> none  [relayout(): lax.all_to_all(block, 'lon', split_axis=3, concat_axis=2, tiled=True)]
    dynamic_slice x76 -> x75, local copies, waits for them, and re-layouts: 142 us -> 143 us  [piece_for(): return lax.dynamic_index_in_dim(tile_blocks, target, axis=1, keepdims=False)]
    another operation x74 -> x73, local copies, waits for them, and re-layouts: 136 us -> 138 us  [relayout(): window = jnp.stack(received[::-1], axis=0)]
  transfers between devices with their start and end apart: 83 -> 96, of which waited for: 8 -> 8; matrix products, arithmetic and copies ran while one was open for 28% -> 24% of each run, Pallas kernels for 0% -> 0%
where the time goes in v1:
time: 928 us; the launch traced here: 912 us
  starting transfers between devices  515 us (55%)
  local copies, waits for them, and re-layouts  370 us (40%)
  waiting for transfers between devices  14 us (2%)
  other arithmetic  10.3 us (1%)
    ppermute x70, starting transfers between devices, from_behind(): return lax.ppermute(shard, axis, pairs)  365 us
    dynamic_slice x75, local copies, waits for them, and re-layouts, piece_for(): return lax.dynamic_index_in_dim(tile_blocks, target, axis=1, keepdims=False)  143 us
    another operation x73, local copies, waits for them, and re-layouts, relayout(): window = jnp.stack(received[::-1], axis=0)  138 us
    ppermute x14, starting transfers between devices, rotated_exchange(): lax.ppermute(sent, axis, [(i, (i + step) % size) for i in range(size)])  133 us
    unnamed x39, local copies, waits for them, and re-layouts  76.7 us
  transfers between devices with their start and end apart: 96, of which 8 were waited for; matrix products, arithmetic and copies ran while one was open for 24% of the time, Pallas kernels for 0%

profile of v1, /device:TPU:24, one launch (start us, length us, event | category | flops | bytes accessed | tf_op | source)
XLA Modules:
  0.0 911.5 jit_solution(9405151069586803916)
XLA Ops:
  27.2 21.1 %collective-permute-start.9 = (f32[1,1,64,16,16]{2,4,0,3,1:T(8,128)S(1)}, f32[1,1,64,16,16]{2,4,0,3,1:T(8,128)S(1)}, u32[]{:S(2)}, u32[]{:S(2)}) collective-permute-start(f32[1,1,64,16,16]{2,4,0,3,1:T(8,128)S(1)} %get-tuple-element.99), channel_id=1, source_target_pairs={{0,4},{1,5},{2,6},{3,7},{4,0},{5,1},{6,2},{7,3},{8,12},{9,13},{10,... | collective-permute-start | bytes 196616 | tf_op jit(solution)/shard_map/ppermute | solution.py:28
  48.3 19.0 %collective-permute-start.10 = (f32[1,1,64,16,16]{2,4,0,3,1:T(8,128)S(1)}, f32[1,1,64,16,16]{2,4,0,3,1:T(8,128)S(1)}, u32[]{:S(2)}, u32[]{:S(2)}) collective-permute-start(f32[1,1,64,16,16]{2,4,0,3,1:T(8,128)S(1)} %get-tuple-element.98), channel_id=1, source_target_pairs={{0,5},{1,6},{2,7},{3,0},{4,1},{5,2},{6,3},{7,4},{8,13},{9,14},{10,... | collective-permute-start | bytes 196616 | tf_op jit(solution)/shard_map/ppermute | solution.py:28
  67.3 19.0 %collective-permute-start.11 = (f32[1,1,64,16,16]{2,4,0,3,1:T(8,128)S(1)}, f32[1,1,64,16,16]{2,4,0,3,1:T(8,128)S(1)}, u32[]{:S(2)}, u32[]{:S(2)}) collective-permute-start(f32[1,1,64,16,16]{2,4,0,3,1:T(8,128)S(1)} %get-tuple-element.97), channel_id=1, source_target_pairs={{0,6},{1,7},{2,0},{3,1},{4,2},{5,3},{6,4},{7,5},{8,14},{9,15},{10,... | collective-permute-start | bytes 196616 | tf_op jit(solution)/shard_map/ppermute | solution.py:28
  91.7 8.4 constant_dynamic-slice_fusion.32
  101.8 9.5 %collective-permute-start.33 = (f32[1,1,128,16]{2,3,1,0:T(8,128)S(1)}, f32[1,1,128,16]{2,3,1,0:T(8,128)S(1)}, u32[]{:S(2)}, u32[]{:S(2)}) collective-permute-start(f32[1,1,128,16]{2,3,1,0:T(8,128)S(1)} %bitcast.349), channel_id=1, source_target_pairs={{16,0},{24,8},{32,16},{40,24},{48,32},{56,40},{64,48},{72,56},{80,... | collective-permute-start | bytes 24584 | tf_op jit(solution)/shard_map/ppermute | solution.py:50
  129.3 9.1 collective-permute-start.37
  149.0 8.2 collective-permute-start.39
  188.5 13.1 %collective-permute-start.48 = (f32[1,1,128,16]{2,3,1,0:T(8,128)S(1)}, f32[1,1,128,16]{2,3,1,0:T(8,128)S(1)}, u32[]{:S(2)}, u32[]{:S(2)}) collective-permute-start(f32[1,1,128,16]{2,3,1,0:T(8,128)S(1)} %bitcast.287), channel_id=1, source_target_pairs={{136,0},{144,8},{152,16},{160,24},{168,32},{176,40},{184,48},{192,... | collective-permute-start | bytes 24584 | tf_op jit(solution)/shard_map/ppermute | solution.py:50
  201.6 19.0 %collective-permute-start.49 = (f32[1,1,128,16]{2,3,1,0:T(8,128)S(1)}, f32[1,1,128,16]{2,3,1,0:T(8,128)S(1)}, u32[]{:S(2)}, u32[]{:S(2)}) collective-permute-start(f32[1,1,128,16]{2,3,1,0:T(8,128)S(1)} %bitcast.281), channel_id=1, source_target_pairs={{144,0},{152,8},{160,16},{168,24},{176,32},{184,40},{192,48},{200,... | collective-permute-start | bytes 24584 | tf_op jit(solution)/shard_map/ppermute | solution.py:50
  220.7 19.0 %collective-permute-start.50 = (f32[1,1,128,16]{2,3,1,0:T(8,128)S(1)}, f32[1,1,128,16]{2,3,1,0:T(8,128)S(1)}, u32[]{:S(2)}, u32[]{:S(2)}) collective-permute-start(f32[1,1,128,16]{2,3,1,0:T(8,128)S(1)} %bitcast.278), channel_id=1, source_target_pairs={{152,0},{160,8},{168,16},{176,24},{184,32},{192,40},{200,48},{208,... | collective-permute-start | bytes 24584 | tf_op jit(solution)/shard_map/ppermute | solution.py:50
  239.7 8.4 constant_dynamic-slice_fusion.50
  257.5 8.6 collective-permute-start.17
  333.4 35.0 %collective-permute-start.13 = (f32[1,1,128,16]{2,3,1,0:T(8,128)S(1)}, f32[1,1,128,16]{2,3,1,0:T(8,128)}, u32[]{:S(2)}, u32[]{:S(2)}) collective-permute-start(f32[1,1,128,16]{2,3,1,0:T(8,128)S(1)} %bitcast.265), channel_id=1, source_target_pairs={{0,152},{8,160},{16,168},{24,176},{32,184},{40,192},{48,200},{56,2... | collective-permute-start | bytes 24584 | tf_op jit(solution)/shard_map/ppermute | solution.py:50
  368.4 19.0 %collective-permute-start.14 = (f32[1,1,128,16]{2,3,1,0:T(8,128)S(1)}, f32[1,1,128,16]{2,3,1,0:T(8,128)}, u32[]{:S(2)}, u32[]{:S(2)}) collective-permute-start(f32[1,1,128,16]{2,3,1,0:T(8,128)S(1)} %bitcast.261), channel_id=1, source_target_pairs={{0,144},{8,152},{16,160},{24,168},{32,176},{40,184},{48,192},{56,2... | collective-permute-start | bytes 24584 | tf_op jit(solution)/shard_map/ppermute | solution.py:50
  387.4 19.0 %collective-permute-start.15 = (f32[1,1,128,16]{2,3,1,0:T(8,128)S(1)}, f32[1,1,128,16]{2,3,1,0:T(8,128)}, u32[]{:S(2)}, u32[]{:S(2)}) collective-permute-start(f32[1,1,128,16]{2,3,1,0:T(8,128)S(1)} %bitcast.259), channel_id=1, source_target_pairs={{0,136},{8,144},{16,152},{24,160},{32,168},{40,176},{48,184},{56,1... | collective-permute-start | bytes 24584 | tf_op jit(solution)/shard_map/ppermute | solution.py:50
  407.6 12.1 %copy.544 = f32[1,1,1,128,16]{0,3,4,2,1:T(8,128)S(1)} copy(f32[1,1,1,128,16]{1,4,3,2,0:T(8,128)S(1)} %get-tuple-element.76) | data formatting | bytes 16384
  472.9 23.2 %stack.256 = f32[39,1,1,128,16]{0,3,4,2,1:T(8,128)} concatenate(f32[1,1,1,128,16]{0,3,4,2,1:T(8,128)} %copy.440, f32[1,1,1,128,16]{0,3,4,2,1:T(8,128)} %copy.441, f32[1,1,1,128,16]{0,3,4,2,1:T(8,128)} %copy.442, f32[1,1,1,128,16]{0,3,4,2,1:T(8,128)} %copy.443, f32[1,1,1,128,16]{0,3,4,2,1:T(8,128)} %copy.444, f32[1,1,1,128,16]{0,3,4,2,1:T(8,128)} %copy.445, ...), dimensions={0} | concatenate | bytes 638976 | tf_op jit(solution)/shard_map/stack | solution.py:101
  496.2 7.2 dynamic_update_slice.55
  526.5 20.5 %collective-permute-start.60 = (f32[1,1,64,16,16]{2,4,0,3,1:T(8,128)S(1)}, f32[1,1,64,16,16]{2,4,0,3,1:T(8,128)S(1)}, u32[]{:S(2)}, u32[]{:S(2)}) collective-permute-start(f32[1,1,64,16,16]{2,4,0,3,1:T(8,128)S(1)} %get-tuple-element.41), channel_id=1, source_target_pairs={{0,4},{1,5},{2,6},{3,7},{4,0},{5,1},{6,2},{7,3},{8,12},{9,13},{10,... | collective-permute-start | bytes 196616 | tf_op jit(solution)/shard_map/ppermute | solution.py:28
  547.0 19.0 %collective-permute-start.61 = (f32[1,1,64,16,16]{2,4,0,3,1:T(8,128)S(1)}, f32[1,1,64,16,16]{2,4,0,3,1:T(8,128)S(1)}, u32[]{:S(2)}, u32[]{:S(2)}) collective-permute-start(f32[1,1,64,16,16]{2,4,0,3,1:T(8,128)S(1)} %get-tuple-element.40), channel_id=1, source_target_pairs={{0,5},{1,6},{2,7},{3,0},{4,1},{5,2},{6,3},{7,4},{8,13},{9,14},{10,... | collective-permute-start | bytes 196616 | tf_op jit(solution)/shard_map/ppermute | solution.py:28
  566.0 19.0 %collective-permute-start.62 = (f32[1,1,64,16,16]{2,4,0,3,1:T(8,128)S(1)}, f32[1,1,64,16,16]{2,4,0,3,1:T(8,128)S(1)}, u32[]{:S(2)}, u32[]{:S(2)}) collective-permute-start(f32[1,1,64,16,16]{2,4,0,3,1:T(8,128)S(1)} %get-tuple-element.39), channel_id=1, source_target_pairs={{0,6},{1,7},{2,0},{3,1},{4,2},{5,3},{6,4},{7,5},{8,14},{9,15},{10,... | collective-permute-start | bytes 196616 | tf_op jit(solution)/shard_map/ppermute | solution.py:28
  590.4 7.5 constant_dynamic-slice_fusion.16
  602.5 8.6 collective-permute-start.65
  716.6 7.8 constant_dynamic-slice_fusion
  739.6 6.4 collective-permute-start.82
  747.6 7.8 collective-permute-start.83
  757.1 8.7 collective-permute-start.84
  767.4 11.9 %collective-permute-start.85 = (f32[1,1,128,16]{2,3,1,0:T(8,128)S(1)}, f32[1,1,128,16]{2,3,1,0:T(8,128)S(1)}, u32[]{:S(2)}, u32[]{:S(2)}) collective-permute-start(f32[1,1,128,16]{2,3,1,0:T(8,128)S(1)} %bitcast.338), channel_id=1, source_target_pairs={{48,0},{56,8},{64,16},{72,24},{80,32},{88,40},{96,48},{104,56},{11... | collective-permute-start | bytes 24584 | tf_op jit(solution)/shard_map/ppermute | solution.py:50
  787.5 9.7 %collective-permute-start.86 = (f32[1,1,128,16]{2,3,1,0:T(8,128)S(1)}, f32[1,1,128,16]{2,3,1,0:T(8,128)S(1)}, u32[]{:S(2)}, u32[]{:S(2)}) collective-permute-start(f32[1,1,128,16]{2,3,1,0:T(8,128)S(1)} %bitcast.327), channel_id=1, source_target_pairs={{56,0},{64,8},{72,16},{80,24},{88,32},{96,40},{104,48},{112,56},{1... | collective-permute-start | bytes 24584 | tf_op jit(solution)/shard_map/ppermute | solution.py:50
  797.2 12.4 %collective-permute-start.87 = (f32[1,1,128,16]{2,3,1,0:T(8,128)S(1)}, f32[1,1,128,16]{2,3,1,0:T(8,128)S(1)}, u32[]{:S(2)}, u32[]{:S(2)}) collective-permute-start(f32[1,1,128,16]{2,3,1,0:T(8,128)S(1)} %bitcast.319), channel_id=1, source_target_pairs={{64,0},{72,8},{80,16},{88,24},{96,32},{104,40},{112,48},{120,56},{... | collective-permute-start | bytes 24584 | tf_op jit(solution)/shard_map/ppermute | solution.py:50
  809.6 10.1 %collective-permute-start.88 = (f32[1,1,128,16]{2,3,1,0:T(8,128)S(1)}, f32[1,1,128,16]{2,3,1,0:T(8,128)S(1)}, u32[]{:S(2)}, u32[]{:S(2)}) collective-permute-start(f32[1,1,128,16]{2,3,1,0:T(8,128)S(1)} %bitcast.315), channel_id=1, source_target_pairs={{72,0},{80,8},{88,16},{96,24},{104,32},{112,40},{120,48},{128,56},... | collective-permute-start | bytes 24584 | tf_op jit(solution)/shard_map/ppermute | solution.py:50
  891.4 19.0 %copy.543 = f32[33,1,1,128,16]{3,4,0,2,1:T(8,128)S(1)} copy(f32[33,1,1,128,16]{1,4,3,2,0:T(8,128)} %constant_dynamic-update-slice_fusion) | data formatting | bytes 540672 | tf_op jit(solution)/shard_map/stack | solution.py:101
  (394 shorter events, 463.2 us)
Async XLA Ops:
  21.9 45.4 %collective-permute-start.6 = (f32[1,1,64,16,16]{2,4,0,3,1:T(8,128)S(1)}, f32[1,1,64,16,16]{2,4,0,3,1:T(8,128)S(1)}, u32[]{:S(2)}, u32[]{:S(2)}) collective-permute-start(f32[1,1,64,16,16]{2,4,0,3,1:T(8,128)S(1)} %get-tuple-element.102), channel_id=1, source_target_pairs={{0,1},{1,2},{2,3},{3,4},{4,5},{5,6},{6,7},{7,0},{8,9},{9,10},{10,1... | collective-permute-start | bytes 196616 | tf_op jit(solution)/shard_map/ppermute | solution.py:28
  22.1 64.2 %collective-permute-start.7 = (f32[1,1,64,16,16]{2,4,0,3,1:T(8,128)S(1)}, f32[1,1,64,16,16]{2,4,0,3,1:T(8,128)S(1)}, u32[]{:S(2)}, u32[]{:S(2)}) collective-permute-start(f32[1,1,64,16,16]{2,4,0,3,1:T(8,128)S(1)} %get-tuple-element.101), channel_id=1, source_target_pairs={{0,2},{1,3},{2,4},{3,5},{4,6},{5,7},{6,0},{7,1},{8,10},{9,11},{10,... | collective-permute-start | bytes 196616 | tf_op jit(solution)/shard_map/ppermute | solution.py:28
  24.0 64.8 %collective-permute-start.8 = (f32[1,1,64,16,16]{2,4,0,3,1:T(8,128)S(1)}, f32[1,1,64,16,16]{2,4,0,3,1:T(8,128)S(1)}, u32[]{:S(2)}, u32[]{:S(2)}) collective-permute-start(f32[1,1,64,16,16]{2,4,0,3,1:T(8,128)S(1)} %get-tuple-element.100), channel_id=1, source_target_pairs={{0,3},{1,4},{2,5},{3,6},{4,7},{5,0},{6,1},{7,2},{8,11},{9,12},{10,... | collective-permute-start | bytes 196616 | tf_op jit(solution)/shard_map/ppermute | solution.py:28
  27.2 61.7 %collective-permute-start.9 = (f32[1,1,64,16,16]{2,4,0,3,1:T(8,128)S(1)}, f32[1,1,64,16,16]{2,4,0,3,1:T(8,128)S(1)}, u32[]{:S(2)}, u32[]{:S(2)}) collective-permute-start(f32[1,1,64,16,16]{2,4,0,3,1:T(8,128)S(1)} %get-tuple-element.99), channel_id=1, source_target_pairs={{0,4},{1,5},{2,6},{3,7},{4,0},{5,1},{6,2},{7,3},{8,12},{9,13},{10,... | collective-permute-start | bytes 196616 | tf_op jit(solution)/shard_map/ppermute | solution.py:28
  48.3 40.6 %collective-permute-start.10 = (f32[1,1,64,16,16]{2,4,0,3,1:T(8,128)S(1)}, f32[1,1,64,16,16]{2,4,0,3,1:T(8,128)S(1)}, u32[]{:S(2)}, u32[]{:S(2)}) collective-permute-start(f32[1,1,64,16,16]{2,4,0,3,1:T(8,128)S(1)} %get-tuple-element.98), channel_id=1, source_target_pairs={{0,5},{1,6},{2,7},{3,0},{4,1},{5,2},{6,3},{7,4},{8,13},{9,14},{10,... | collective-permute-start | bytes 196616 | tf_op jit(solution)/shard_map/ppermute | solution.py:28
  101.8 41.6 %collective-permute-start.33 = (f32[1,1,128,16]{2,3,1,0:T(8,128)S(1)}, f32[1,1,128,16]{2,3,1,0:T(8,128)S(1)}, u32[]{:S(2)}, u32[]{:S(2)}) collective-permute-start(f32[1,1,128,16]{2,3,1,0:T(8,128)S(1)} %bitcast.349), channel_id=1, source_target_pairs={{16,0},{24,8},{32,16},{40,24},{48,32},{56,40},{64,48},{72,56},{80,... | collective-permute-start | bytes 24584 | tf_op jit(solution)/shard_map/ppermute | solution.py:50
  125.8 44.0 %collective-permute-start.36 = (f32[1,1,128,16]{2,3,1,0:T(8,128)S(1)}, f32[1,1,128,16]{2,3,1,0:T(8,128)S(1)}, u32[]{:S(2)}, u32[]{:S(2)}) collective-permute-start(f32[1,1,128,16]{2,3,1,0:T(8,128)S(1)} %bitcast.335), channel_id=1, source_target_pairs={{40,0},{48,8},{56,16},{64,24},{72,32},{80,40},{88,48},{96,56},{104... | collective-permute-start | bytes 24584 | tf_op jit(solution)/shard_map/ppermute | solution.py:50
  129.3 42.3 %collective-permute-start.37 = (f32[1,1,128,16]{2,3,1,0:T(8,128)S(1)}, f32[1,1,128,16]{2,3,1,0:T(8,128)S(1)}, u32[]{:S(2)}, u32[]{:S(2)}) collective-permute-start(f32[1,1,128,16]{2,3,1,0:T(8,128)S(1)} %bitcast.333), channel_id=1, source_target_pairs={{48,0},{56,8},{64,16},{72,24},{80,32},{88,40},{96,48},{104,56},{11... | collective-permute-start | bytes 24584 | tf_op jit(solution)/shard_map/ppermute | solution.py:50
  177.5 43.2 %collective-permute-start.45 = (f32[1,1,128,16]{2,3,1,0:T(8,128)S(1)}, f32[1,1,128,16]{2,3,1,0:T(8,128)S(1)}, u32[]{:S(2)}, u32[]{:S(2)}) collective-permute-start(f32[1,1,128,16]{2,3,1,0:T(8,128)S(1)} %bitcast.250), channel_id=1, source_target_pairs={{112,0},{120,8},{128,16},{136,24},{144,32},{152,40},{160,48},{168,... | collective-permute-start | bytes 24584 | tf_op jit(solution)/shard_map/ppermute | solution.py:50
  185.3 71.0 %collective-permute-start.46 = (f32[1,1,128,16]{2,3,1,0:T(8,128)S(1)}, f32[1,1,128,16]{2,3,1,0:T(8,128)S(1)}, u32[]{:S(2)}, u32[]{:S(2)}) collective-permute-start(f32[1,1,128,16]{2,3,1,0:T(8,128)S(1)} %bitcast.305), channel_id=1, source_target_pairs={{120,0},{128,8},{136,16},{144,24},{152,32},{160,40},{168,48},{176,... | collective-permute-start | bytes 24584 | tf_op jit(solution)/shard_map/ppermute | solution.py:50
  187.2 70.4 %collective-permute-start.47 = (f32[1,1,128,16]{2,3,1,0:T(8,128)S(1)}, f32[1,1,128,16]{2,3,1,0:T(8,128)S(1)}, u32[]{:S(2)}, u32[]{:S(2)}) collective-permute-start(f32[1,1,128,16]{2,3,1,0:T(8,128)S(1)} %bitcast.295), channel_id=1, source_target_pairs={{128,0},{136,8},{144,16},{152,24},{160,32},{168,40},{176,48},{184,... | collective-permute-start | bytes 24584 | tf_op jit(solution)/shard_map/ppermute | solution.py:50
  188.5 77.7 %collective-permute-start.48 = (f32[1,1,128,16]{2,3,1,0:T(8,128)S(1)}, f32[1,1,128,16]{2,3,1,0:T(8,128)S(1)}, u32[]{:S(2)}, u32[]{:S(2)}) collective-permute-start(f32[1,1,128,16]{2,3,1,0:T(8,128)S(1)} %bitcast.287), channel_id=1, source_target_pairs={{136,0},{144,8},{152,16},{160,24},{168,32},{176,40},{184,48},{192,... | collective-permute-start | bytes 24584 | tf_op jit(solution)/shard_map/ppermute | solution.py:50
  201.6 66.5 %collective-permute-start.49 = (f32[1,1,128,16]{2,3,1,0:T(8,128)S(1)}, f32[1,1,128,16]{2,3,1,0:T(8,128)S(1)}, u32[]{:S(2)}, u32[]{:S(2)}) collective-permute-start(f32[1,1,128,16]{2,3,1,0:T(8,128)S(1)} %bitcast.281), channel_id=1, source_target_pairs={{144,0},{152,8},{160,16},{168,24},{176,32},{184,40},{192,48},{200,... | collective-permute-start | bytes 24584 | tf_op jit(solution)/shard_map/ppermute | solution.py:50
  220.7 49.4 %collective-permute-start.50 = (f32[1,1,128,16]{2,3,1,0:T(8,128)S(1)}, f32[1,1,128,16]{2,3,1,0:T(8,128)S(1)}, u32[]{:S(2)}, u32[]{:S(2)}) collective-permute-start(f32[1,1,128,16]{2,3,1,0:T(8,128)S(1)} %bitcast.278), channel_id=1, source_target_pairs={{152,0},{160,8},{168,16},{176,24},{184,32},{192,40},{200,48},{208,... | collective-permute-start | bytes 24584 | tf_op jit(solution)/shard_map/ppermute | solution.py:50
  311.5 56.9 %collective-permute-start.29 = (f32[1,1,128,16]{2,3,1,0:T(8,128)}, f32[1,1,128,16]{2,3,1,0:T(8,128)S(1)}, u32[]{:S(2)}, u32[]{:S(2)}) collective-permute-start(f32[1,1,128,16]{2,3,1,0:T(8,128)} %bitcast.56), channel_id=1, source_target_pairs={{0,24},{8,32},{16,40},{24,48},{32,56},{40,64},{48,72},{56,80},{64,... | collective-permute-start | bytes 24584 | tf_op jit(solution)/shard_map/ppermute | solution.py:50
  314.0 73.5 %collective-permute-start.30 = (f32[1,1,128,16]{2,3,1,0:T(8,128)}, f32[1,1,128,16]{2,3,1,0:T(8,128)S(1)}, u32[]{:S(2)}, u32[]{:S(2)}) collective-permute-start(f32[1,1,128,16]{2,3,1,0:T(8,128)} %bitcast.58), channel_id=1, source_target_pairs={{0,16},{8,24},{16,32},{24,40},{32,48},{40,56},{48,64},{56,72},{64,... | collective-permute-start | bytes 24584 | tf_op jit(solution)/shard_map/ppermute | solution.py:50
  325.4 137.2 %collective-permute-start.31 = (f32[1,1,128,16]{2,3,1,0:T(8,128)S(1)}, f32[1,1,128,16]{2,3,1,0:T(8,128)}, u32[]{:S(2)}, u32[]{:S(2)}) collective-permute-start(f32[1,1,128,16]{2,3,1,0:T(8,128)S(1)} %bitcast.271), channel_id=1, source_target_pairs={{0,8},{8,16},{16,24},{24,32},{32,40},{40,48},{48,56},{56,64},{64,7... | collective-permute-start | bytes 24584 | tf_op jit(solution)/shard_map/ppermute | solution.py:50
  327.9 136.8 %collective-permute-start.32 = (f32[1,1,128,16]{2,3,1,0:T(8,128)S(1)}, f32[1,1,128,16]{2,3,1,0:T(8,128)}, u32[]{:S(2)}, u32[]{:S(2)}) collective-permute-start(f32[1,1,128,16]{2,3,1,0:T(8,128)S(1)} %bitcast.268), channel_id=1, source_target_pairs={{8,0},{16,8},{24,16},{32,24},{40,32},{48,40},{56,48},{64,56},{72,6... | collective-permute-start | bytes 24584 | tf_op jit(solution)/shard_map/ppermute | solution.py:50
  333.4 133.3 %collective-permute-start.13 = (f32[1,1,128,16]{2,3,1,0:T(8,128)S(1)}, f32[1,1,128,16]{2,3,1,0:T(8,128)}, u32[]{:S(2)}, u32[]{:S(2)}) collective-permute-start(f32[1,1,128,16]{2,3,1,0:T(8,128)S(1)} %bitcast.265), channel_id=1, source_target_pairs={{0,152},{8,160},{16,168},{24,176},{32,184},{40,192},{48,200},{56,2... | collective-permute-start | bytes 24584 | tf_op jit(solution)/shard_map/ppermute | solution.py:50
  368.4 100.4 %collective-permute-start.14 = (f32[1,1,128,16]{2,3,1,0:T(8,128)S(1)}, f32[1,1,128,16]{2,3,1,0:T(8,128)}, u32[]{:S(2)}, u32[]{:S(2)}) collective-permute-start(f32[1,1,128,16]{2,3,1,0:T(8,128)S(1)} %bitcast.261), channel_id=1, source_target_pairs={{0,144},{8,152},{16,160},{24,168},{32,176},{40,184},{48,192},{56,2... | collective-permute-start | bytes 24584 | tf_op jit(solution)/shard_map/ppermute | solution.py:50
  387.4 83.4 %collective-permute-start.15 = (f32[1,1,128,16]{2,3,1,0:T(8,128)S(1)}, f32[1,1,128,16]{2,3,1,0:T(8,128)}, u32[]{:S(2)}, u32[]{:S(2)}) collective-permute-start(f32[1,1,128,16]{2,3,1,0:T(8,128)S(1)} %bitcast.259), channel_id=1, source_target_pairs={{0,136},{8,144},{16,152},{24,160},{32,168},{40,176},{48,184},{56,1... | collective-permute-start | bytes 24584 | tf_op jit(solution)/shard_map/ppermute | solution.py:50
  521.4 44.6 %collective-permute-start.57 = (f32[1,1,64,16,16]{2,4,0,3,1:T(8,128)S(1)}, f32[1,1,64,16,16]{2,4,0,3,1:T(8,128)S(1)}, u32[]{:S(2)}, u32[]{:S(2)}) collective-permute-start(f32[1,1,64,16,16]{2,4,0,3,1:T(8,128)S(1)} %get-tuple-element.44), channel_id=1, source_target_pairs={{0,1},{1,2},{2,3},{3,4},{4,5},{5,6},{6,7},{7,0},{8,9},{9,10},{10,1... | collective-permute-start | bytes 196616 | tf_op jit(solution)/shard_map/ppermute | solution.py:28
  521.4 63.6 %collective-permute-start.58 = (f32[1,1,64,16,16]{2,4,0,3,1:T(8,128)S(1)}, f32[1,1,64,16,16]{2,4,0,3,1:T(8,128)S(1)}, u32[]{:S(2)}, u32[]{:S(2)}) collective-permute-start(f32[1,1,64,16,16]{2,4,0,3,1:T(8,128)S(1)} %get-tuple-element.43), channel_id=1, source_target_pairs={{0,2},{1,3},{2,4},{3,5},{4,6},{5,7},{6,0},{7,1},{8,10},{9,11},{10,... | collective-permute-start | bytes 196616 | tf_op jit(solution)/shard_map/ppermute | solution.py:28
  523.4 64.2 %collective-permute-start.59 = (f32[1,1,64,16,16]{2,4,0,3,1:T(8,128)S(1)}, f32[1,1,64,16,16]{2,4,0,3,1:T(8,128)S(1)}, u32[]{:S(2)}, u32[]{:S(2)}) collective-permute-start(f32[1,1,64,16,16]{2,4,0,3,1:T(8,128)S(1)} %get-tuple-element.42), channel_id=1, source_target_pairs={{0,3},{1,4},{2,5},{3,6},{4,7},{5,0},{6,1},{7,2},{8,11},{9,12},{10,... | collective-permute-start | bytes 196616 | tf_op jit(solution)/shard_map/ppermute | solution.py:28
  526.5 61.1 %collective-permute-start.60 = (f32[1,1,64,16,16]{2,4,0,3,1:T(8,128)S(1)}, f32[1,1,64,16,16]{2,4,0,3,1:T(8,128)S(1)}, u32[]{:S(2)}, u32[]{:S(2)}) collective-permute-start(f32[1,1,64,16,16]{2,4,0,3,1:T(8,128)S(1)} %get-tuple-element.41), channel_id=1, source_target_pairs={{0,4},{1,5},{2,6},{3,7},{4,0},{5,1},{6,2},{7,3},{8,12},{9,13},{10,... | collective-permute-start | bytes 196616 | tf_op jit(solution)/shard_map/ppermute | solution.py:28
  726.1 41.4 %collective-permute-start.80 = (f32[1,1,128,16]{2,3,1,0:T(8,128)S(1)}, f32[1,1,128,16]{2,3,1,0:T(8,128)S(1)}, u32[]{:S(2)}, u32[]{:S(2)}) collective-permute-start(f32[1,1,128,16]{2,3,1,0:T(8,128)S(1)} %bitcast.351), channel_id=1, source_target_pairs={{8,0},{16,8},{24,16},{32,24},{40,32},{48,40},{56,48},{64,56},{72,6... | collective-permute-start | bytes 24584 | tf_op jit(solution)/shard_map/ppermute | solution.py:50
  733.2 54.3 %collective-permute-start.81 = (f32[1,1,128,16]{2,3,1,0:T(8,128)S(1)}, f32[1,1,128,16]{2,3,1,0:T(8,128)S(1)}, u32[]{:S(2)}, u32[]{:S(2)}) collective-permute-start(f32[1,1,128,16]{2,3,1,0:T(8,128)S(1)} %bitcast.346), channel_id=1, source_target_pairs={{16,0},{24,8},{32,16},{40,24},{48,32},{56,40},{64,48},{72,56},{80,... | collective-permute-start | bytes 24584 | tf_op jit(solution)/shard_map/ppermute | solution.py:50
  739.6 57.6 %collective-permute-start.82 = (f32[1,1,128,16]{2,3,1,0:T(8,128)S(1)}, f32[1,1,128,16]{2,3,1,0:T(8,128)S(1)}, u32[]{:S(2)}, u32[]{:S(2)}) collective-permute-start(f32[1,1,128,16]{2,3,1,0:T(8,128)S(1)} %bitcast.344), channel_id=1, source_target_pairs={{24,0},{32,8},{40,16},{48,24},{56,32},{64,40},{72,48},{80,56},{88,... | collective-permute-start | bytes 24584 | tf_op jit(solution)/shard_map/ppermute | solution.py:50
  747.6 62.0 %collective-permute-start.83 = (f32[1,1,128,16]{2,3,1,0:T(8,128)S(1)}, f32[1,1,128,16]{2,3,1,0:T(8,128)S(1)}, u32[]{:S(2)}, u32[]{:S(2)}) collective-permute-start(f32[1,1,128,16]{2,3,1,0:T(8,128)S(1)} %bitcast.342), channel_id=1, source_target_pairs={{32,0},{40,8},{48,16},{56,24},{64,32},{72,40},{80,48},{88,56},{96,... | collective-permute-start | bytes 24584 | tf_op jit(solution)/shard_map/ppermute | solution.py:50
  757.1 62.6 %collective-permute-start.84 = (f32[1,1,128,16]{2,3,1,0:T(8,128)S(1)}, f32[1,1,128,16]{2,3,1,0:T(8,128)S(1)}, u32[]{:S(2)}, u32[]{:S(2)}) collective-permute-start(f32[1,1,128,16]{2,3,1,0:T(8,128)S(1)} %bitcast.340), channel_id=1, source_target_pairs={{40,0},{48,8},{56,16},{64,24},{72,32},{80,40},{88,48},{96,56},{104... | collective-permute-start | bytes 24584 | tf_op jit(solution)/shard_map/ppermute | solution.py:50
  767.4 54.4 %collective-permute-start.85 = (f32[1,1,128,16]{2,3,1,0:T(8,128)S(1)}, f32[1,1,128,16]{2,3,1,0:T(8,128)S(1)}, u32[]{:S(2)}, u32[]{:S(2)}) collective-permute-start(f32[1,1,128,16]{2,3,1,0:T(8,128)S(1)} %bitcast.338), channel_id=1, source_target_pairs={{48,0},{56,8},{64,16},{72,24},{80,32},{88,40},{96,48},{104,56},{11... | collective-permute-start | bytes 24584 | tf_op jit(solution)/shard_map/ppermute | solution.py:50
  787.5 42.0 %collective-permute-start.86 = (f32[1,1,128,16]{2,3,1,0:T(8,128)S(1)}, f32[1,1,128,16]{2,3,1,0:T(8,128)S(1)}, u32[]{:S(2)}, u32[]{:S(2)}) collective-permute-start(f32[1,1,128,16]{2,3,1,0:T(8,128)S(1)} %bitcast.327), channel_id=1, source_target_pairs={{56,0},{64,8},{72,16},{80,24},{88,32},{96,40},{104,48},{112,56},{1... | collective-permute-start | bytes 24584 | tf_op jit(solution)/shard_map/ppermute | solution.py:50
  (67 other events, 1524.1 us)
